TPU v7x, 512 devices: a whole 4x8x8 slice. The times are simulated.
512 devices in a mesh: grp: 128 (over z, y, core), col: 4 (over x).
Axes of the slice: x: 4, y: 8, z: 8, core: 2. Of those that a mesh axis runs over, the one named last changes fastest.
Arguments:
- points: float32 [65536, 1024], P(('grp', 'col')), may hold values from -1000 to 1000
- labels: int32 [65536], P(('grp', 'col')), may hold values from 0 to 31, as said below
- boundaries: int32 [33], replicated, may hold values from 0 to 128, as said below
- centroids: float32 [128, 512, 1024], P('grp', 'col'), may hold values from -12 to 12, as said below
Outputs:
- centroid_table: float32 [128, 512, 1024], P('grp', 'col')
Inputs may be any that keep to these rules, and one draw needn't show every extreme that they name: `labels`: on each device's rows, the rows that name parent p number at most 2 times the number of grp indices in p's group; on every device some parent reaches this. boundaries[0] = 0 and boundaries[32] = 128; every group has 1 to 7 grp indices, and some group has 7. `centroids`: rows of the table at grp indices of one parent's group are equal.
All inputs are finite; a program needn't handle non-finite values.
Results may differ from a plain program's by a relative error of at most 0.0003.
Values sent between devices are 32-bit elements; how exact they have to be, the bound alone decides.
A program may use at most 64 MiB of HBM per device.

v0:
```python
import jax
import jax.numpy as jnp
from jax import lax
from jax.sharding import PartitionSpec as P

ITERS = 2


SHARPNESS = 6.0
HIGHEST = lax.Precision.HIGHEST


def passed_along(block, axis, distance):
    devices = range(lax.axis_size(axis))
    route = [(i - distance, i) for i in devices if i - distance in devices]
    return lax.ppermute(block, axis, route)


def destinations(row_labels, boundaries, slots):
    row_count = row_labels.shape[0]
    parents = boundaries.shape[0] - 1
    one_hot = row_labels[:, None] == jnp.arange(parents, dtype=jnp.int32)[None, :]
    starts = jnp.sum(jnp.where(one_hot, boundaries[None, :-1], 0), axis=1)
    positions = jnp.arange(row_count, dtype=jnp.int32)
    before = (row_labels[:, None] == row_labels[None, :]) & (
        positions[None, :] < positions[:, None]
    )
    ranking = jnp.sum(before.astype(jnp.int32), axis=1)
    return (starts + ranking // slots, ranking % slots)


def segmented(earlier, later):
    keep = later[0] > 0.5
    return (
        jnp.maximum(earlier[0], later[0]),
        jnp.where(keep, later[1], earlier[1] + later[1]),
        jnp.where(keep, later[2], earlier[2] + later[2]),
    )


def on_device(points, labels, boundaries, centroids):
    groups = lax.axis_size("grp")
    col_count = lax.axis_size("col")
    rows_dev = points.shape[0]
    width = points.shape[1]
    slots = 2 * rows_dev // groups
    my_index = lax.axis_index("grp")
    my_parent = jnp.sum((boundaries[1:] <= my_index).astype(jnp.int32))
    group_first = boundaries[my_parent]
    group_last = boundaries[my_parent + 1] - 1

    def block_route(block_labels):
        return destinations(block_labels, boundaries, slots)

    whole, whole_labels = (
        lax.all_gather(points, "col", axis=0, tiled=True),
        lax.all_gather(labels.astype(jnp.float32), "col", axis=0, tiled=True),
    )
    label_blocks = whole_labels.astype(jnp.int32).reshape(col_count, rows_dev)
    targets, seats = jax.vmap(block_route)(label_blocks)
    seats = seats + jnp.arange(col_count, dtype=jnp.int32)[:, None] * slots
    flat_index = (targets * (col_count * slots) + seats).reshape(-1)
    buffer = jnp.zeros((groups * col_count * slots, width), jnp.float32).at[flat_index].set(whole)
    marks = jnp.zeros((groups * col_count * slots,), jnp.float32).at[flat_index].set(1.0)
    received, flags = (
        lax.all_to_all(
            buffer.reshape(groups, col_count * slots, width),
            "grp",
            split_axis=0,
            concat_axis=0,
            tiled=True,
        ),
        lax.all_to_all(
            marks.reshape(groups, col_count * slots), "grp", split_axis=0, concat_axis=0, tiled=True
        ),
    )
    row_block = received.reshape(-1, width)
    row_weights = flags.reshape(-1)
    current = centroids[0]
    start_flag = jnp.where(my_index == group_first, 1.0, 0.0).astype(jnp.float32).reshape(1)
    end_flag = jnp.where(my_index == group_last, 1.0, 0.0).astype(jnp.float32).reshape(1)
    score_scale = SHARPNESS / width
    for iteration in range(ITERS):
        half_norm = 0.5 * jnp.sum(current * current, axis=1)
        logits = (
            jnp.dot(row_block, current.T, precision=HIGHEST) - half_norm[None, :]
        ) * score_scale
        peak_value = lax.pmax(jnp.max(logits, axis=1), "col")
        raised = jnp.exp(logits - peak_value[:, None])
        totals = lax.psum(jnp.sum(raised, axis=1), "col")
        shares = raised * (row_weights / totals)[:, None]
        weighted = lax.dot_general(shares, row_block, (((0,), (0,)), ((), ())), precision=HIGHEST)
        mass_sum = jnp.sum(shares, axis=0)
        forward = (start_flag, weighted, mass_sum)
        backward = (end_flag, weighted, mass_sum)
        for level in range(3):
            incoming = passed_along((forward[0], forward[1], forward[2]), "grp", 1 << level)
            forward = segmented(incoming, forward)
        for level in range(3):
            incoming = passed_along((backward[0], backward[1], backward[2]), "grp", -(1 << level))
            backward = segmented(incoming, backward)
        full_weighted = forward[1] + backward[1] - weighted
        full_mass = forward[2] + backward[2] - mass_sum
        current = (full_weighted + current) / (full_mass + 1.0)[:, None]
    return current[None]


def solution(mesh):
    placed = (P(("grp", "col"), None), P(("grp", "col")), P(), P("grp", "col", None))
    return jax.shard_map(
        on_device, mesh=mesh, in_specs=placed, out_specs=P("grp", "col", None), check_vma=False
    )
```

profile of v0, /device:TPU:256, one launch (start us, length us, event | category | flops | bytes accessed | tf_op | source)
XLA Modules:
  0.0 399.8 jit_solution(5482505985042954472)
XLA Ops:
  7.9 9.7 %all-gather = f32[4,1,128]{2,1,0:T(1,128)S(1)} all-gather(f32[1,1,128]{2,1,0:T(1,128)S(1)} %convert_bitcast_fusion), channel_id=1, replica_groups=mesh['grp'=128,'col'=4] {'col'}, dimensions={0}, use_global_device_ids=true | all-gather | bytes 2560 | tf_op jit(solution)/shard_map/all_gather | solution.py:57
  22.6 14.2 %all-to-all-start.1 = ((f32[128,1,8]{2,1,0:T(1,128)}), f32[128,1,8]{2,1,0:T(1,128)S(1)}, u32[]{:S(2)}, u32[]{:S(2)}) async-start(f32[128,1,8]{2,1,0:T(1,128)} %bitcast.14), calls=%async_computation.1 | async-start | bytes 131072 | tf_op jit(solution)/shard_map/all_to_all | solution.py:73
  36.8 10.6 %all-gather.3.cloned.1.call-done = f32[512,1024]{1,0:T(8,128)} async-done(((f32[128,1024]{1,0:T(8,128)}), f32[512,1024]{1,0:T(8,128)}) %all-gather.3.cloned.1.call-update) | async-done | bytes 2097168 | tf_op jit(solution)/shard_map/all_gather | solution.py:56
  47.4 5.5 %scatter_custom_fusion = f32[1024,1024]{1,0:T(8,128)} fusion(s32[512]{0:T(512)S(1)} %bitcast.60, f32[512,1024]{1,0:T(8,128)} %all-gather.3.cloned.1.call-done, f32[]{:T(128)} %constant.51.clone.1), kind=kCustom, calls=%fused_computation.10 | custom fusion | bytes 4194816 | tf_op jit(solution)/shard_map/scatter | solution.py:63
  52.9 14.4 %all-to-all-start = ((f32[128,8,1024]{2,1,0:T(8,128)}), f32[128,8,1024]{2,1,0:T(8,128)}, u32[]{:S(2)}, u32[]{:S(2)}) async-start(f32[128,8,1024]{2,1,0:T(8,128)} %bitcast.53), calls=%async_computation | async-start | bytes 8388608 | tf_op jit(solution)/shard_map/all_to_all | solution.py:66
  68.8 91.9 %all-to-all-done = f32[128,8,1024]{2,1,0:T(8,128)} async-done(((f32[128,8,1024]{2,1,0:T(8,128)}), f32[128,8,1024]{2,1,0:T(8,128)}, u32[]{:S(2)}, u32[]{:S(2)}) %all-to-all-start) | async-done | bytes 4194336 | tf_op jit(solution)/shard_map/all_to_all | solution.py:66
  160.7 6.6 %fusion.54 = (f32[1024]{0:T(1024)S(1)}, f32[1024,128]{0,1:T(8,128)S(1)}) fusion(f32[128]{0:T(128)S(1)} %broadcast_multiply_fusion.1, f32[1,128,1024]{2,1,0:T(8,128)S(1)} %copy-done, f32[128,8,1024]{2,1,0:T(8,128)} %all-to-all-done), kind=kOutput, calls=%fused_computation.92 | convolution fusion | flops 1611004928 | bytes 5247488 | tf_op jit(solution)/shard_map/dot_general | solution.py:86
  167.3 8.6 %pmax.14 = f32[1024]{0:T(1024)S(1)} all-reduce(f32[1024]{0:T(1024)S(1)} %get-tuple-element.19), channel_id=1, replica_groups=mesh['grp'=128,'col'=4] {'col'}, use_global_device_ids=true, to_apply=%region_6.7 | all-reduce | flops 1024 | bytes 8192 | tf_op jit(solution)/shard_map/pmax | solution.py:88
  176.0 8.9 %psum.14 = f32[1024]{0:T(1024)S(1)} all-reduce(f32[1024]{0:T(1024)S(1)} %fusion.35), channel_id=1, replica_groups=mesh['grp'=128,'col'=4] {'col'}, use_global_device_ids=true, to_apply=%region_9.10 | all-reduce | flops 1024 | bytes 8192 | tf_op jit(solution)/shard_map/psum | solution.py:90
  191.5 7.0 %collective-permute-start.7 = (f32[128,1024]{1,0:T(8,128)S(1)}, f32[128,1024]{1,0:T(8,128)S(1)}, u32[]{:S(2)}, u32[]{:S(2)}) collective-permute-start(f32[128,1024]{1,0:T(8,128)S(1)} %fusion.4), channel_id=1, source_target_pairs={{4,0},{8,4},{12,8},{16,12},{20,16},{24,20},{28,24},{32,28},{36,32}... | collective-permute-start | bytes 1572872 | tf_op jit(solution)/shard_map/ppermute | solution.py:16
  207.2 7.2 %collective-permute-start.8 = (f32[128,1024]{1,0:T(8,128)S(1)}, f32[128,1024]{1,0:T(8,128)S(1)}, u32[]{:S(2)}, u32[]{:S(2)}) collective-permute-start(f32[128,1024]{1,0:T(8,128)S(1)} %get-tuple-element.10), channel_id=1, source_target_pairs={{8,0},{12,4},{16,8},{20,12},{24,16},{28,20},{32,24},{36,28},{40,32... | collective-permute-start | bytes 1572872 | tf_op jit(solution)/shard_map/ppermute | solution.py:16
  216.5 7.0 %collective-permute-start.13 = (f32[128]{0:T(128)S(1)}, f32[128]{0:T(128)S(1)}, u32[]{:S(2)}, u32[]{:S(2)}) collective-permute-start(f32[128]{0:T(128)S(1)} %multiply_reduce_fusion.2), channel_id=1, source_target_pairs={{4,0},{8,4},{12,8},{16,12},{20,16},{24,20},{28,24},{32,28},{36,32}... | collective-permute-start | bytes 1544 | tf_op jit(solution)/shard_map/ppermute | solution.py:16
  226.2 5.4 %collective-permute-done = f32[1]{0:T(128)} collective-permute-done((f32[1]{0:T(128)}, f32[1]{0:T(128)}, u32[]{:S(2)}, u32[]{:S(2)}) %collective-permute-start) | collective-permute-done | bytes 36 | tf_op jit(solution)/shard_map/ppermute | solution.py:16
  238.2 7.2 %collective-permute-start.14 = (f32[128]{0:T(128)S(1)}, f32[128]{0:T(128)S(1)}, u32[]{:S(2)}, u32[]{:S(2)}) collective-permute-start(f32[128]{0:T(128)S(1)} %get-tuple-element.14), channel_id=1, source_target_pairs={{8,0},{12,4},{16,8},{20,12},{24,16},{28,20},{32,24},{36,28},{40,32... | collective-permute-start | bytes 1544 | tf_op jit(solution)/shard_map/ppermute | solution.py:16
  247.6 8.1 %collective-permute-start.9 = (f32[128,1024]{1,0:T(8,128)S(1)}, f32[128,1024]{1,0:T(8,128)S(1)}, u32[]{:S(2)}, u32[]{:S(2)}) collective-permute-start(f32[128,1024]{1,0:T(8,128)S(1)} %add_select_fusion.7), channel_id=1, source_target_pairs={{16,0},{20,4},{24,8},{28,12},{32,16},{36,20},{40,24},{44,28},{48,3... | collective-permute-start | bytes 1572872 | tf_op jit(solution)/shard_map/ppermute | solution.py:16
  257.7 8.1 %collective-permute-start.15 = (f32[128]{0:T(128)S(1)}, f32[128]{0:T(128)S(1)}, u32[]{:S(2)}, u32[]{:S(2)}) collective-permute-start(f32[128]{0:T(128)S(1)} %broadcast_select_fusion.3), channel_id=1, source_target_pairs={{16,0},{20,4},{24,8},{28,12},{32,16},{36,20},{40,24},{44,28},{48,3... | collective-permute-start | bytes 1544 | tf_op jit(solution)/shard_map/ppermute | solution.py:16
  284.6 6.6 %fusion.55 = (f32[1024]{0:T(1024)S(1)}, f32[1024,128]{0,1:T(8,128)S(1)}) fusion(f32[128]{0:T(128)S(1)} %broadcast_multiply_fusion, f32[128,1024]{1,0:T(8,128)S(1)} %get-tuple-element.6, f32[128,8,1024]{2,1,0:T(8,128)} %all-to-all-done), kind=kOutput, calls=%fused_computation.93 | convolution fusion | flops 1611004928 | bytes 5247488 | tf_op jit(solution)/shard_map/dot_general | solution.py:86
  291.3 8.6 %pmax.15 = f32[1024]{0:T(1024)S(1)} all-reduce(f32[1024]{0:T(1024)S(1)} %get-tuple-element.21), channel_id=1, replica_groups=mesh['grp'=128,'col'=4] {'col'}, use_global_device_ids=true, to_apply=%region_13.14 | all-reduce | flops 1024 | bytes 8192 | tf_op jit(solution)/shard_map/pmax | solution.py:88
  299.9 8.9 %psum.15 = f32[1024]{0:T(1024)S(1)} all-reduce(f32[1024]{0:T(1024)S(1)} %fusion.36), channel_id=1, replica_groups=mesh['grp'=128,'col'=4] {'col'}, use_global_device_ids=true, to_apply=%region_15.16 | all-reduce | flops 1024 | bytes 8192 | tf_op jit(solution)/shard_map/psum | solution.py:90
  315.4 7.0 %collective-permute-start.19 = (f32[128,1024]{1,0:T(8,128)S(1)}, f32[128,1024]{1,0:T(8,128)S(1)}, u32[]{:S(2)}, u32[]{:S(2)}) collective-permute-start(f32[128,1024]{1,0:T(8,128)S(1)} %fusion), channel_id=1, source_target_pairs={{4,0},{8,4},{12,8},{16,12},{20,16},{24,20},{28,24},{32,28},{36,32}... | collective-permute-start | bytes 1572872 | tf_op jit(solution)/shard_map/ppermute | solution.py:16
  340.5 6.6 %collective-permute-start.25 = (f32[128]{0:T(128)S(1)}, f32[128]{0:T(128)S(1)}, u32[]{:S(2)}, u32[]{:S(2)}) collective-permute-start(f32[128]{0:T(128)S(1)} %multiply_reduce_fusion.1), channel_id=1, source_target_pairs={{4,0},{8,4},{12,8},{16,12},{20,16},{24,20},{28,24},{32,28},{36,32}... | collective-permute-start | bytes 1544 | tf_op jit(solution)/shard_map/ppermute | solution.py:16
  353.1 7.2 %collective-permute-start.26 = (f32[128]{0:T(128)S(1)}, f32[128]{0:T(128)S(1)}, u32[]{:S(2)}, u32[]{:S(2)}) collective-permute-start(f32[128]{0:T(128)S(1)} %get-tuple-element.12), channel_id=1, source_target_pairs={{8,0},{12,4},{16,8},{20,12},{24,16},{28,20},{32,24},{36,28},{40,32... | collective-permute-start | bytes 1544 | tf_op jit(solution)/shard_map/ppermute | solution.py:16
  369.2 8.1 %collective-permute-start.27 = (f32[128]{0:T(128)S(1)}, f32[128]{0:T(128)S(1)}, u32[]{:S(2)}, u32[]{:S(2)}) collective-permute-start(f32[128]{0:T(128)S(1)} %broadcast_select_fusion.2), channel_id=1, source_target_pairs={{16,0},{20,4},{24,8},{28,12},{32,16},{36,20},{40,24},{44,28},{48,3... | collective-permute-start | bytes 1544 | tf_op jit(solution)/shard_map/ppermute | solution.py:16
  377.4 14.4 %collective-permute-done.24 = f32[128]{0:T(128)S(1)} collective-permute-done((f32[128]{0:T(128)S(1)}, f32[128]{0:T(128)S(1)}, u32[]{:S(2)}, u32[]{:S(2)}) %collective-permute-start.24) | collective-permute-done | bytes 544 | tf_op jit(solution)/shard_map/ppermute | solution.py:16
  (94 shorter events, 91.2 us)
Async XLA Ops:
  6.5 40.9 %all-gather.3.cloned.1.call-start = ((), (), s32[]{:S(2)}) async-start(), calls=%async_computation.2 | async-start | bytes 2621440 | tf_op jit(solution)/shard_map/all_gather | solution.py:56
  22.6 30.2 %all-to-all-start.1 = ((f32[128,1,8]{2,1,0:T(1,128)}), f32[128,1,8]{2,1,0:T(1,128)S(1)}, u32[]{:S(2)}, u32[]{:S(2)}) async-start(f32[128,1,8]{2,1,0:T(1,128)} %bitcast.14), calls=%async_computation.1 | async-start | bytes 131072 | tf_op jit(solution)/shard_map/all_to_all | solution.py:73
  52.9 107.8 %all-to-all-start = ((f32[128,8,1024]{2,1,0:T(8,128)}), f32[128,8,1024]{2,1,0:T(8,128)}, u32[]{:S(2)}, u32[]{:S(2)}) async-start(f32[128,8,1024]{2,1,0:T(8,128)} %bitcast.53), calls=%async_computation | async-start | bytes 8388608 | tf_op jit(solution)/shard_map/all_to_all | solution.py:66
  189.6 13.8 %collective-permute-start.2 = (f32[128,1024]{1,0:T(8,128)S(1)}, f32[128,1024]{1,0:T(8,128)S(1)}, u32[]{:S(2)}, u32[]{:S(2)}) collective-permute-start(f32[128,1024]{1,0:T(8,128)S(1)} %fusion.4), channel_id=1, source_target_pairs={{0,4},{4,8},{8,12},{12,16},{16,20},{20,24},{24,28},{28,32},{32,36}... | collective-permute-start | bytes 1572872 | tf_op jit(solution)/shard_map/ppermute | solution.py:16
  205.3 40.2 %collective-permute-start.3 = (f32[128,1024]{1,0:T(8,128)S(1)}, f32[128,1024]{1,0:T(8,128)S(1)}, u32[]{:S(2)}, u32[]{:S(2)}) collective-permute-start(f32[128,1024]{1,0:T(8,128)S(1)} %get-tuple-element.9), channel_id=1, source_target_pairs={{0,8},{4,12},{8,16},{12,20},{16,24},{20,28},{24,32},{28,36},{32,40... | collective-permute-start | bytes 1572872 | tf_op jit(solution)/shard_map/ppermute | solution.py:16
  207.2 40.3 %collective-permute-start.8 = (f32[128,1024]{1,0:T(8,128)S(1)}, f32[128,1024]{1,0:T(8,128)S(1)}, u32[]{:S(2)}, u32[]{:S(2)}) collective-permute-start(f32[128,1024]{1,0:T(8,128)S(1)} %get-tuple-element.10), channel_id=1, source_target_pairs={{8,0},{12,4},{16,8},{20,12},{24,16},{28,20},{32,24},{36,28},{40,32... | collective-permute-start | bytes 1572872 | tf_op jit(solution)/shard_map/ppermute | solution.py:16
  214.6 21.6 %collective-permute-start.10 = (f32[128]{0:T(128)S(1)}, f32[128]{0:T(128)S(1)}, u32[]{:S(2)}, u32[]{:S(2)}) collective-permute-start(f32[128]{0:T(128)S(1)} %multiply_reduce_fusion.2), channel_id=1, source_target_pairs={{0,4},{4,8},{8,12},{12,16},{16,20},{20,24},{24,28},{28,32},{32,36}... | collective-permute-start | bytes 1544 | tf_op jit(solution)/shard_map/ppermute | solution.py:16
  216.5 19.7 %collective-permute-start.13 = (f32[128]{0:T(128)S(1)}, f32[128]{0:T(128)S(1)}, u32[]{:S(2)}, u32[]{:S(2)}) collective-permute-start(f32[128]{0:T(128)S(1)} %multiply_reduce_fusion.2), channel_id=1, source_target_pairs={{4,0},{8,4},{12,8},{16,12},{20,16},{24,20},{28,24},{32,28},{36,32}... | collective-permute-start | bytes 1544 | tf_op jit(solution)/shard_map/ppermute | solution.py:16
  236.3 19.4 %collective-permute-start.11 = (f32[128]{0:T(128)S(1)}, f32[128]{0:T(128)S(1)}, u32[]{:S(2)}, u32[]{:S(2)}) collective-permute-start(f32[128]{0:T(128)S(1)} %get-tuple-element.13), channel_id=1, source_target_pairs={{0,8},{4,12},{8,16},{12,20},{16,24},{20,28},{24,32},{28,36},{32,40... | collective-permute-start | bytes 1544 | tf_op jit(solution)/shard_map/ppermute | solution.py:16
  238.2 19.5 %collective-permute-start.14 = (f32[128]{0:T(128)S(1)}, f32[128]{0:T(128)S(1)}, u32[]{:S(2)}, u32[]{:S(2)}) collective-permute-start(f32[128]{0:T(128)S(1)} %get-tuple-element.14), channel_id=1, source_target_pairs={{8,0},{12,4},{16,8},{20,12},{24,16},{28,20},{32,24},{36,28},{40,32... | collective-permute-start | bytes 1544 | tf_op jit(solution)/shard_map/ppermute | solution.py:16
  245.5 38.7 %collective-permute-start.4 = (f32[128,1024]{1,0:T(8,128)S(1)}, f32[128,1024]{1,0:T(8,128)S(1)}, u32[]{:S(2)}, u32[]{:S(2)}) collective-permute-start(f32[128,1024]{1,0:T(8,128)S(1)} %add_select_fusion.10), channel_id=1, source_target_pairs={{0,16},{4,20},{8,24},{12,28},{16,32},{20,36},{24,40},{28,44},{32,4... | collective-permute-start | bytes 1572872 | tf_op jit(solution)/shard_map/ppermute | solution.py:16
  247.6 36.7 %collective-permute-start.9 = (f32[128,1024]{1,0:T(8,128)S(1)}, f32[128,1024]{1,0:T(8,128)S(1)}, u32[]{:S(2)}, u32[]{:S(2)}) collective-permute-start(f32[128,1024]{1,0:T(8,128)S(1)} %add_select_fusion.7), channel_id=1, source_target_pairs={{16,0},{20,4},{24,8},{28,12},{32,16},{36,20},{40,24},{44,28},{48,3... | collective-permute-start | bytes 1572872 | tf_op jit(solution)/shard_map/ppermute | solution.py:16
  255.7 28.5 %collective-permute-start.12 = (f32[128]{0:T(128)S(1)}, f32[128]{0:T(128)S(1)}, u32[]{:S(2)}, u32[]{:S(2)}) collective-permute-start(f32[128]{0:T(128)S(1)} %broadcast_select_fusion.9), channel_id=1, source_target_pairs={{0,16},{4,20},{8,24},{12,28},{16,32},{20,36},{24,40},{28,44},{32,4... | collective-permute-start | bytes 1544 | tf_op jit(solution)/shard_map/ppermute | solution.py:16
  257.7 26.5 %collective-permute-start.15 = (f32[128]{0:T(128)S(1)}, f32[128]{0:T(128)S(1)}, u32[]{:S(2)}, u32[]{:S(2)}) collective-permute-start(f32[128]{0:T(128)S(1)} %broadcast_select_fusion.3), channel_id=1, source_target_pairs={{16,0},{20,4},{24,8},{28,12},{32,16},{36,20},{40,24},{44,28},{48,3... | collective-permute-start | bytes 1544 | tf_op jit(solution)/shard_map/ppermute | solution.py:16
  313.5 13.8 %collective-permute-start.16 = (f32[128,1024]{1,0:T(8,128)S(1)}, f32[128,1024]{1,0:T(8,128)S(1)}, u32[]{:S(2)}, u32[]{:S(2)}) collective-permute-start(f32[128,1024]{1,0:T(8,128)S(1)} %fusion), channel_id=1, source_target_pairs={{0,4},{4,8},{8,12},{12,16},{16,20},{20,24},{24,28},{28,32},{32,36}... | collective-permute-start | bytes 1572872 | tf_op jit(solution)/shard_map/ppermute | solution.py:16
  329.2 31.1 %collective-permute-start.20 = (f32[128,1024]{1,0:T(8,128)S(1)}, f32[128,1024]{1,0:T(8,128)S(1)}, u32[]{:S(2)}, u32[]{:S(2)}) collective-permute-start(f32[128,1024]{1,0:T(8,128)S(1)} %get-tuple-element.7), channel_id=1, source_target_pairs={{8,0},{12,4},{16,8},{20,12},{24,16},{28,20},{32,24},{36,28},{40,32... | collective-permute-start | bytes 1572872 | tf_op jit(solution)/shard_map/ppermute | solution.py:16
  331.1 31.2 %collective-permute-start.17 = (f32[128,1024]{1,0:T(8,128)S(1)}, f32[128,1024]{1,0:T(8,128)S(1)}, u32[]{:S(2)}, u32[]{:S(2)}) collective-permute-start(f32[128,1024]{1,0:T(8,128)S(1)} %get-tuple-element.8), channel_id=1, source_target_pairs={{0,8},{4,12},{8,16},{12,20},{16,24},{20,28},{24,32},{28,36},{32,40... | collective-permute-start | bytes 1572872 | tf_op jit(solution)/shard_map/ppermute | solution.py:16
  335.2 15.9 %collective-permute-start.22 = (f32[128]{0:T(128)S(1)}, f32[128]{0:T(128)S(1)}, u32[]{:S(2)}, u32[]{:S(2)}) collective-permute-start(f32[128]{0:T(128)S(1)} %multiply_reduce_fusion.1), channel_id=1, source_target_pairs={{0,4},{4,8},{8,12},{12,16},{16,20},{20,24},{24,28},{28,32},{32,36}... | collective-permute-start | bytes 1544 | tf_op jit(solution)/shard_map/ppermute | solution.py:16
  351.1 16.1 %collective-permute-start.23 = (f32[128]{0:T(128)S(1)}, f32[128]{0:T(128)S(1)}, u32[]{:S(2)}, u32[]{:S(2)}) collective-permute-start(f32[128]{0:T(128)S(1)} %get-tuple-element.11), channel_id=1, source_target_pairs={{0,8},{4,12},{8,16},{12,20},{16,24},{20,28},{24,32},{28,36},{32,40... | collective-permute-start | bytes 1544 | tf_op jit(solution)/shard_map/ppermute | solution.py:16
  353.1 16.1 %collective-permute-start.26 = (f32[128]{0:T(128)S(1)}, f32[128]{0:T(128)S(1)}, u32[]{:S(2)}, u32[]{:S(2)}) collective-permute-start(f32[128]{0:T(128)S(1)} %get-tuple-element.12), channel_id=1, source_target_pairs={{8,0},{12,4},{16,8},{20,12},{24,16},{28,20},{32,24},{36,28},{40,32... | collective-permute-start | bytes 1544 | tf_op jit(solution)/shard_map/ppermute | solution.py:16
  360.4 31.4 %collective-permute-start.21 = (f32[128,1024]{1,0:T(8,128)S(1)}, f32[128,1024]{1,0:T(8,128)S(1)}, u32[]{:S(2)}, u32[]{:S(2)}) collective-permute-start(f32[128,1024]{1,0:T(8,128)S(1)} %add_select_fusion.1), channel_id=1, source_target_pairs={{16,0},{20,4},{24,8},{28,12},{32,16},{36,20},{40,24},{44,28},{48,3... | collective-permute-start | bytes 1572872 | tf_op jit(solution)/shard_map/ppermute | solution.py:16
  362.4 29.4 %collective-permute-start.18 = (f32[128,1024]{1,0:T(8,128)S(1)}, f32[128,1024]{1,0:T(8,128)S(1)}, u32[]{:S(2)}, u32[]{:S(2)}) collective-permute-start(f32[128,1024]{1,0:T(8,128)S(1)} %add_select_fusion.4), channel_id=1, source_target_pairs={{0,16},{4,20},{8,24},{12,28},{16,32},{20,36},{24,40},{28,44},{32,4... | collective-permute-start | bytes 1572872 | tf_op jit(solution)/shard_map/ppermute | solution.py:16
  367.3 24.5 %collective-permute-start.24 = (f32[128]{0:T(128)S(1)}, f32[128]{0:T(128)S(1)}, u32[]{:S(2)}, u32[]{:S(2)}) collective-permute-start(f32[128]{0:T(128)S(1)} %broadcast_select_fusion.8), channel_id=1, source_target_pairs={{0,16},{4,20},{8,24},{12,28},{16,32},{20,36},{24,40},{28,44},{32,4... | collective-permute-start | bytes 1544 | tf_op jit(solution)/shard_map/ppermute | solution.py:16
  369.2 22.6 %collective-permute-start.27 = (f32[128]{0:T(128)S(1)}, f32[128]{0:T(128)S(1)}, u32[]{:S(2)}, u32[]{:S(2)}) collective-permute-start(f32[128]{0:T(128)S(1)} %broadcast_select_fusion.2), channel_id=1, source_target_pairs={{16,0},{20,4},{24,8},{28,12},{32,16},{36,20},{40,24},{44,28},{48,3... | collective-permute-start | bytes 1544 | tf_op jit(solution)/shard_map/ppermute | solution.py:16
  (9 other events, 116.1 us)
Sparse Core Ops, SparseCore 0:
  9.5 37.8 all-gather.2
where the time goes:
time: 401 us; the launch traced here: 400 us
  starting transfers between devices  151 us (38%)
  waiting for transfers between devices  145 us (36%)
  blocking collectives  44.7 us (11%)
  matrix products  22.5 us (6%)
  between operations  20.7 us (5%)
  local copies, waits for them, and re-layouts  9.92 us (2%)
  other arithmetic  5.98 us (1%)
    ppermute x28, starting transfers between devices, passed_along(): return lax.ppermute(block, axis, route)  123 us
    all_to_all x1, waiting for transfers between devices, on_device(): lax.all_to_all(buffer.reshape(groups, col_count * slots, width), 'grp', s...  91.9 us
    ppermute x28, waiting for transfers between devices, passed_along(): return lax.ppermute(block, axis, route)  41.6 us
    psum x2, blocking collectives, on_device(): totals = lax.psum(jnp.sum(raised, axis=1), 'col')  17.8 us
    pmax x2, blocking collectives, on_device(): peak_value = lax.pmax(jnp.max(logits, axis=1), 'col')  17.2 us
    all_to_all x1, starting transfers between devices, on_device(): lax.all_to_all(buffer.reshape(groups, col_count * slots, width), 'grp', s...  14.4 us
    all_to_all x1, starting transfers between devices, on_device(): lax.all_to_all(marks.reshape(groups, col_count * slots), 'grp', split_axi...  14.2 us
    dot_general x2, matrix products, on_device(): jnp.dot(row_block, current.T, precision=HIGHEST) - half_norm[None, :]  13.3 us
  transfers between devices with their start and end apart: 31, of which 11 were waited for; matrix products, arithmetic and copies ran while one was open for 3% of the time, Pallas kernels for 0%

commit v1 on v0

v1 whole, which is shorter than its diff:
```python
import functools

import jax
import jax.numpy as jnp
from jax import lax
from jax.experimental import pallas as pl
from jax.experimental.pallas import tpu as pltpu
from jax.sharding import PartitionSpec as P

ITERS = 2
SHARPNESS = 6.0
HIGHEST = lax.Precision.HIGHEST
MESH = pl.DeviceIdType.MESH
LANES = 128
SEATS = 2
MARK = 4096.0
ROUNDS = 3
WINDOW = 3
CHUNK = 256
F32 = jnp.float32
BF16 = jnp.bfloat16


def plane_shape(groups):
    chips = groups // 2
    side = 1
    while side * side < chips:
        side *= 2
    return chips // side, side


def peer(me, offset, shape):
    nz, ny = shape
    core, y, z = me % 2, (me // 2) % ny, me // (2 * ny)
    k, dz, dc = offset // (2 * nz), (offset // 2) % nz, offset % 2
    dy = (k + dz) % ny
    return (((z + dz) % nz) * ny + (y + dy) % ny) * 2 + (core + dc) % 2


def halves(x):
    hi = x.astype(BF16)
    return hi, (x - hi.astype(F32)).astype(BF16)


def dot_nt(a, b):
    return lax.dot_general(a, b, (((1,), (1,)), ((), ())), preferred_element_type=F32)


def dot_nn(a, b):
    return lax.dot_general(a, b, (((1,), (0,)), ((), ())), preferred_element_type=F32)


def kernel(
    groups, cols, bounds_ref, labels_ref, points_ref, cent_ref, out_ref,
    seats_ref, rows_ref, xh_ref, xl_ref, logit_ref, valid_ref, share_ref, code_ref, stat_ref,
    w_ref, i_ref, j_ref, t_ref, rr_ref, rl_ref, sr_ref, sl_ref,
    cw_ref, ci_ref, cj_ref, ct_ref, crr_ref, crl_ref, csr_ref, csl_ref,
    send_sem, recv_sem, local_sem, fan_sem, right_sem, left_sem, relay_sem, far_sem,
    stat_send, stat_recv, pair_send, pair_recv, chain_send, chain_recv,
):
    shape = plane_shape(groups)
    nz, ny = shape
    parts = ny
    rows_dev, width = points_ref.shape
    kids = cent_ref.shape[0]
    half_kids = kids // 2
    tile = width // LANES
    chunks = width // CHUNK
    block = SEATS * tile
    seat_count = groups * SEATS
    part_rows = 2 * nz * block
    all_rows = cols * seat_count
    score_scale = SHARPNESS / width
    me = lax.axis_index("grp")
    col = lax.axis_index("col")
    core = me % 2
    sibling = me + 1 - 2 * core
    ahead = lax.rem(me + 2, groups)
    behind = lax.rem(me + groups - 2, groups)
    right, left = lax.rem(col + 1, cols), lax.rem(col + cols - 1, cols)
    far = lax.rem(col + 2, cols)

    barrier = pltpu.get_barrier_semaphore()

    def greet(o, carry):
        pl.semaphore_signal(barrier, inc=1, device_id=(peer(me, o, shape), col), device_id_type=MESH)
        return carry

    lax.fori_loop(1, groups, greet, 0)
    for other in (right, left, far):
        pl.semaphore_signal(barrier, inc=1, device_id=(me, other), device_id_type=MESH)

    labels = jnp.broadcast_to(labels_ref[...], (rows_dev, rows_dev))
    r = lax.broadcasted_iota(jnp.int32, (rows_dev, rows_dev), 0)
    c = lax.broadcasted_iota(jnp.int32, (rows_dev, rows_dev), 1)
    before = (labels == labels.T) & (r < c)
    rank = jnp.sum(before.astype(F32), axis=0, keepdims=True)
    mine = labels_ref[...]
    first = jnp.zeros_like(mine)
    for p in range(bounds_ref.shape[0] - 1):
        first = jnp.where(mine == p, bounds_ref[p].astype(F32), first)
    seat = (first * SEATS + rank).astype(jnp.int32)
    s = lax.broadcasted_iota(jnp.int32, (seat_count, rows_dev), 0)
    pick = (s == jnp.broadcast_to(seat, (seat_count, rows_dev))).astype(F32)
    empty = 1.0 - jnp.sum(pick, axis=1, keepdims=True)
    lane = lax.broadcasted_iota(jnp.int32, (seat_count, LANES), 1)
    for q in range(tile):
        part = jnp.dot(pick, points_ref[:, q * LANES : (q + 1) * LANES], precision=HIGHEST)
        if q == 0:
            part = part + jnp.where(lane == 0, empty * MARK, 0.0)
        seats_ref[pl.ds(q, seat_count, stride=tile), :] = part

    pl.semaphore_wait(barrier, groups - 1 + 3)

    def place(k, source, lo, size):
        base = (k * cols + source) * part_rows + lo
        return rows_ref.at[pl.ds(pl.multiple_of(base, 8), size), :]

    def own_copy():
        return pltpu.make_async_copy(
            seats_ref.at[pl.ds(pl.multiple_of(me * block, block), block), :],
            place(0, col, 0, block),
            local_sem,
        )

    def send(o, carry):
        to = peer(me, o, shape)
        k = o // (2 * nz)
        pltpu.make_async_remote_copy(
            src_ref=seats_ref.at[pl.ds(pl.multiple_of(to * block, block), block), :],
            dst_ref=place(k, col, (o % (2 * nz)) * block, block),
            send_sem=send_sem,
            recv_sem=recv_sem.at[k],
            device_id=(to, col),
            device_id_type=MESH,
        ).start()
        return carry

    def link(src, dst, ssem, rsem, to):
        return pltpu.make_async_remote_copy(
            src_ref=src, dst_ref=dst, send_sem=ssem, recv_sem=rsem,
            device_id=to, device_id_type=MESH,
        )

    half = part_rows // 2

    def to_right(k, source):
        cut = place(k, source, 0, part_rows)
        return link(cut, cut, fan_sem.at[0, k], right_sem.at[k], (me, right))

    def to_left(k, source):
        cut = place(k, source, 0, part_rows)
        return link(cut, cut, fan_sem.at[1, k], left_sem.at[k], (me, left))

    def on_right(k, source):
        cut = place(k, source, 0, half)
        return link(cut, cut, relay_sem.at[0, k], far_sem.at[0, k], (me, right))

    def on_left(k, source):
        cut = place(k, source, half, half)
        return link(cut, cut, relay_sem.at[1, k], far_sem.at[1, k], (me, left))

    def arrived(k):
        lo = block if k == 0 else 0
        cut = place(k, col, lo, part_rows - lo)
        link(cut, cut, send_sem, recv_sem.at[k], (me, right)).wait_recv()

    def relay(k):
        to_right(k, left).wait_recv()
        on_right(k, left).start()
        to_left(k, right).wait_recv()
        on_left(k, right).start()

    def settled(k):
        on_right(k, far).wait_recv()
        on_left(k, far).wait_recv()

    def encode(d, block_of_c):
        hi, lo = halves(block_of_c)
        code_ref[d, :kids, :] = hi
        code_ref[d, kids:, :] = lo

    def score(d, lo, size):
        a = dot_nt(code_ref[d], xh_ref[d, lo : lo + size, :])
        b = dot_nt(code_ref[d, :kids, :], xl_ref[d, lo : lo + size, :])
        return a[:kids] + a[kids:] + b

    pick_mark = (
        (lax.broadcasted_iota(jnp.int32, (16, CHUNK), 0) == 0)
        & (lax.broadcasted_iota(jnp.int32, (16, CHUNK), 1) == 0)
    ).astype(BF16)
    batch = 2 * cols * part_rows // tile

    def absorb(b):
        lo = b * batch
        for q in range(tile):
            hi, rest = halves(rows_ref[pl.ds(lo * tile + q, batch, stride=tile), :])
            d, at = q // (CHUNK // LANES), (q % (CHUNK // LANES)) * LANES
            xh_ref[d, lo : lo + batch, at : at + LANES] = hi
            xl_ref[d, lo : lo + batch, at : at + LANES] = rest
        total = score(0, lo, batch)
        for d in range(1, chunks):
            total = total + score(d, lo, batch)
        logit_ref[:, lo : lo + batch] = total
        mark = dot_nt(pick_mark, xh_ref[0, lo : lo + batch, :])[0:1]
        valid_ref[:, lo : lo + batch] = (mark < 0.5 * MARK).astype(F32)

    own_copy().start()
    lax.fori_loop(1, WINDOW * 2 * nz, send, 0)
    own_copy().wait()
    half_norm = jnp.zeros((kids, 1), F32)
    for d in range(chunks):
        now = cent_ref[:, d * CHUNK : (d + 1) * CHUNK]
        encode(d, now)
        half_norm = half_norm + 0.5 * jnp.sum(now * now, axis=1, keepdims=True)

    for k in range(parts):
        arrived(k)
        to_right(k, col).start()
        to_left(k, col).start()
        if k + WINDOW < parts:
            lax.fori_loop((k + WINDOW) * 2 * nz, (k + WINDOW + 1) * 2 * nz, send, 0)
        if k >= 1:
            relay(k - 1)
        if k >= 3 and k % 2 == 1:
            settled(k - 3)
            settled(k - 2)
            absorb((k - 3) // 2)
    relay(parts - 1)
    settled(parts - 2)
    settled(parts - 1)
    absorb(parts // 2 - 1)

    chip = me // 2

    def owner(g):
        count = jnp.zeros((), jnp.int32)
        for p in range(1, bounds_ref.shape[0]):
            count = count + (bounds_ref[p] <= g).astype(jnp.int32)
        return count

    owner0, owner1 = owner(2 * chip), owner(2 * chip + 1)
    same = (owner0 == owner1).astype(F32)
    from_left = ((owner(2 * chip - 1) == owner0) & (chip > 0)).astype(F32)
    from_right = (owner(2 * chip + 2) == owner1).astype(F32)
    through_left, through_right = same * from_left, same * from_right
    is0 = core == 0
    mine_left = jnp.where(is0, from_left, through_left)
    mine_right = jnp.where(is0, through_right, from_right)
    other_left = jnp.where(is0, through_left, from_left)
    other_right = jnp.where(is0, from_right, through_right)
    my_half = pl.multiple_of(core * half_kids, half_kids)
    its_half = pl.multiple_of((1 - core) * half_kids, half_kids)

    for it in range(ITERS):
        peak = jnp.full((1, all_rows), -jnp.inf, F32)
        logits = (logit_ref[...] - half_norm) * score_scale
        peak = jnp.max(logits, axis=0, keepdims=True)
        raised = jnp.exp(logits - peak)
        logit_ref[...] = raised
        stat_ref[it, 0, 0:1, :] = peak
        stat_ref[it, 0, 1:2, :] = jnp.sum(raised, axis=0, keepdims=True)
        stats = [
            link(stat_ref.at[it, 0], stat_ref.at[it, 1 + n], stat_send.at[it, n], stat_recv.at[it, n], (me, to))
            for n, to in enumerate((right, left, far))
        ]
        for copy in stats:
            copy.start()
        for copy in stats:
            copy.wait()
        top = peak
        for n in range(3):
            top = jnp.maximum(top, stat_ref[it, 1 + n, 0:1, :])
        denominator = jnp.zeros((1, all_rows), F32)
        for n in range(4):
            denominator = denominator + stat_ref[it, n, 1:2, :] * jnp.exp(stat_ref[it, n, 0:1, :] - top)
        scale = valid_ref[...] * jnp.exp(peak - top) / denominator
        shares = logit_ref[...] * scale
        hi, lo = halves(shares)
        share_ref[:kids, :] = hi
        share_ref[kids:, :] = lo
        cw_ref[it, 0] = jnp.broadcast_to(jnp.sum(shares, axis=1, keepdims=True), (kids, LANES))

        def bufs(n):
            if n == 0:
                refs = (cw_ref, ci_ref, cj_ref, ct_ref, crr_ref, crl_ref, csr_ref, csl_ref)
                return [ref.at[it, 0] for ref in refs]
            refs = (w_ref, i_ref, j_ref, t_ref, rr_ref, rl_ref, sr_ref, sl_ref)
            return [ref.at[it, n - 1] for ref in refs]

        def swap(n):
            w, i = bufs(n)[:2]
            return link(w.at[pl.ds(its_half, half_kids), :], i, pair_send.at[it, 0, n], pair_recv.at[it, 0, n], (sibling, col))

        def swap_back(n):
            j, t = bufs(n)[2:4]
            return link(t, j, pair_send.at[it, 1, n], pair_recv.at[it, 1, n], (sibling, col))

        def shift_right(n, m):
            b = bufs(n)
            return link(b[6].at[m], b[4].at[m], chain_send.at[it, 0, n, m], chain_recv.at[it, 0, n, m], (ahead, col))

        def shift_left(n, m):
            b = bufs(n)
            return link(b[7].at[m], b[5].at[m], chain_send.at[it, 1, n, m], chain_recv.at[it, 1, n, m], (behind, col))

        def begin(n):
            swap(n).wait_recv()
            b = bufs(n)
            own, its = b[0][pl.ds(my_half, half_kids), :], b[1][...]
            b[7][0] = jnp.where(is0, own + same * its, its + same * own)
            b[6][0] = jnp.where(is0, its + same * own, own + same * its)
            shift_right(n, 0).start()
            shift_left(n, 0).start()

        swap(0).start()
        for d in range(chunks):
            both = dot_nn(share_ref[...], xh_ref[d])
            rest = dot_nn(share_ref[:kids, :], xl_ref[d])
            w_ref[it, d] = both[:kids] + both[kids:] + rest
            swap(d + 1).start()
            begin(d)
        begin(chunks)
        for m in range(ROUNDS - 1):
            for n in range(chunks + 1):
                b = bufs(n)
                shift_right(n, m).wait_recv()
                b[6][m + 1] = b[6][0] + through_left * b[4][m]
                shift_right(n, m + 1).start()
                shift_left(n, m).wait_recv()
                b[7][m + 1] = b[7][0] + through_right * b[5][m]
                shift_left(n, m + 1).start()
        for n in range(chunks + 1):
            b = bufs(n)
            shift_right(n, ROUNDS - 1).wait_recv()
            shift_left(n, ROUNDS - 1).wait_recv()
            from_l, from_r = b[4][ROUNDS - 1], b[5][ROUNDS - 1]
            toward0, toward1 = b[7][0], b[6][0]
            b[3][...] = jnp.where(is0, toward1, toward0) + other_left * from_l + other_right * from_r
            swap_back(n).start()
            b[0][pl.ds(my_half, half_kids), :] = (
                jnp.where(is0, toward0, toward1) + mine_left * from_l + mine_right * from_r
            )
        swap(0).wait_send()
        swap_back(0).wait_recv()
        cw_ref[it, 0, pl.ds(its_half, half_kids), :] = cj_ref[it, 0]
        shrink = 1.0 / (cw_ref[it, 0] + 1.0)
        shrink = jnp.concatenate([shrink] * (CHUNK // LANES), axis=1)
        source = cent_ref if it == 0 else out_ref
        half_norm = jnp.zeros((kids, 1), F32)
        for d in range(chunks):
            swap(d + 1).wait_send()
            swap_back(d + 1).wait_recv()
            w_ref[it, d, pl.ds(its_half, half_kids), :] = j_ref[it, d]
            at = slice(d * CHUNK, (d + 1) * CHUNK)
            now = (w_ref[it, d] + source[:, at]) * shrink
            out_ref[:, at] = now
            if it + 1 < ITERS:
                encode(d, now)
                half_norm = half_norm + 0.5 * jnp.sum(now * now, axis=1, keepdims=True)
                for b in range(all_rows // batch):
                    lo = b * batch
                    scored = score(d, lo, batch)
                    if d > 0:
                        scored = scored + logit_ref[:, lo : lo + batch]
                    logit_ref[:, lo : lo + batch] = scored
        for n in range(chunks + 1):
            swap_back(n).wait_send()
            for m in range(ROUNDS):
                shift_right(n, m).wait_send()
                shift_left(n, m).wait_send()

    for k in range(parts):
        to_right(k, col).wait_send()
        to_left(k, col).wait_send()
        on_right(k, left).wait_send()
        on_left(k, right).wait_send()
    sent = seats_ref.at[pl.ds(0, (groups - 1) * block), :]
    link(sent, sent, send_sem, recv_sem.at[0], (me, right)).wait_send()


def on_device(points, labels, boundaries, centroids):
    groups = lax.axis_size("grp")
    cols = lax.axis_size("col")
    rows, width = points.shape
    kids = centroids.shape[1]
    tile = width // LANES
    parts = plane_shape(groups)[1]
    seat_count = groups * SEATS
    all_rows = cols * seat_count
    chunks = width // CHUNK
    dma = pltpu.SemaphoreType.DMA
    vmem = pl.BlockSpec(memory_space=pltpu.VMEM)

    def sums_scratch(count, lanes):
        half = kids // 2
        one = pltpu.VMEM((ITERS, count, half, lanes), F32)
        many = pltpu.VMEM((ITERS, count, ROUNDS, half, lanes), F32)
        return [pltpu.VMEM((ITERS, count, kids, lanes), F32), one, one, one, many, many, many, many]

    out = pl.pallas_call(
        functools.partial(kernel, groups, cols),
        out_shape=jax.ShapeDtypeStruct((kids, width), F32),
        in_specs=[pl.BlockSpec(memory_space=pltpu.SMEM), vmem, vmem, vmem],
        out_specs=vmem,
        scratch_shapes=[
            pltpu.VMEM((seat_count * tile, LANES), F32),
            pltpu.VMEM((all_rows * tile, LANES), F32),
            pltpu.VMEM((chunks, all_rows, CHUNK), BF16),
            pltpu.VMEM((chunks, all_rows, CHUNK), BF16),
            pltpu.VMEM((kids, all_rows), F32),
            pltpu.VMEM((1, all_rows), F32),
            pltpu.VMEM((2 * kids, all_rows), BF16),
            pltpu.VMEM((chunks, 2 * kids, CHUNK), BF16),
            pltpu.VMEM((ITERS, 4, 2, all_rows), F32),
            *sums_scratch(chunks, CHUNK),
            *sums_scratch(1, LANES),
            dma, dma((parts,)), dma, dma((2, parts)), dma((parts,)), dma((parts,)),
            dma((2, parts)), dma((2, parts)),
            dma((ITERS, 3)), dma((ITERS, 3)),
            dma((ITERS, 2, chunks + 1)), dma((ITERS, 2, chunks + 1)),
            dma((ITERS, 2, chunks + 1, ROUNDS)), dma((ITERS, 2, chunks + 1, ROUNDS)),
        ],
        compiler_params=pltpu.CompilerParams(
            collective_id=0, has_side_effects=True, vmem_limit_bytes=48 << 20
        ),
    )(boundaries, labels.astype(F32).reshape(1, rows), points, centroids[0])
    return out[None]


def solution(mesh):
    placed = (P(("grp", "col"), None), P(("grp", "col")), P(), P("grp", "col", None))
    return jax.shard_map(
        on_device, mesh=mesh, in_specs=placed, out_specs=P("grp", "col", None), check_vma=False
    )
```

time: 401 us -> 135 us (0.34)
  the two profiles are of different devices: /device:TPU:256 before, /device:TPU:1 now
where the time goes in v1:
time: 135 us
  Pallas kernels  131 us (97%)
  local copies, waits for them, and re-layouts  4.18 us (3%)
    pallas_call x1, Pallas kernels, on_device(): pl.pallas_call(functools.partial(kernel, groups, cols), out_shape=jax.Sha...  131 us
    unnamed x9, local copies, waits for them, and re-layouts  4.18 us

profile of v1, /device:TPU:1, one launch (start us, length us, event | category | flops | bytes accessed | tf_op | source)
XLA Modules:
  0.0 135.1 jit_solution(16059073183375987736)
XLA Ops:
  0.0 0.0 copy-start.3
  0.0 0.7 copy-done.3
  0.7 0.0 copy-start.2
  0.7 0.7 copy-done.2
  1.3 0.0 copy-start
  1.3 1.0 copy-done
  2.4 0.0 copy-start.1
  2.4 1.0 copy-done.1
  3.4 130.9 %shard_map.46 = f32[128,1024]{1,0:T(8,128)S(1)} custom-call(s32[33]{0:T(128)S(1)} %copy-done.2, f32[1,128]{1,0:T(1,128)S(1)} %convert_bitcast_fusion.labels_ref, f32[128,1024]{1,0:T(8,128)S(1)} %copy-done, f32[128,1024]{1,0:T(8,128)S(1)} %bitcast.5), custom_call_target="tpu_custom_call" | custom-call | tf_op jit(solution)/shard_map/pallas_call | solution.py:401
  134.3 0.8 copy.6
  (1 shorter events, 0.0 us)
Async XLA Ops:
  0.0 0.7 copy-start.3
  0.7 0.7 copy-start.2
  1.3 1.0 copy-start
  2.4 1.0 copy-start.1

commit v2 on v1

v2 whole, which is shorter than its diff:
```python
import functools

import jax
import jax.numpy as jnp
from jax import lax
from jax.experimental import pallas as pl
from jax.experimental.pallas import tpu as pltpu
from jax.sharding import PartitionSpec as P

ITERS = 2
SHARPNESS = 6.0
HIGHEST = lax.Precision.HIGHEST
MESH = pl.DeviceIdType.MESH
LANES = 128
SEATS = 2
MARK = 4096.0
ROUNDS = 3
WINDOW = 3
CHUNK = 256
F32 = jnp.float32
BF16 = jnp.bfloat16


def plane_side(groups):
    side = 1
    while 2 * side * side < groups:
        side *= 2
    return side


def part_steps(k, side):
    return 2 * side if k == 0 else 2 * (side - 1)


def part_first(k, side):
    return 0 if k == 0 else 2 * side + 2 * (side - 1) * (k - 1)


def peer(me, k, step, side):
    core, y, z = me % 2, (me // 2) % side, me // (2 * side)
    j, dc = step // 2, step % 2
    if k == 0:
        dz, dy = j, 0
    elif k == 1:
        dz, dy = 0, j + 1
    else:
        dz, dy = j + 1, 1 + (j + k - 2) % (side - 1)
    return (((z + dz) % side) * side + (y + dy) % side) * 2 + (core + dc) % 2


def tour_place(me, target, side):
    shift = side.bit_length()
    core, y, z = me % 2, (me // 2) % side, me // (2 * side)
    dc = (target - core) & 1
    dy = (lax.shift_right_logical(target, 1) - y) & (side - 1)
    dz = (lax.shift_right_logical(target, shift) - z) & (side - 1)
    turn = dy - dz + jnp.where(dy < dz, side - 1, 0)
    rest = 2 * side + 2 * (side - 1) * (1 + turn) + 2 * (dz - 1) + dc
    return jnp.where(dy == 0, 2 * dz + dc, jnp.where(dz == 0, 2 * side + 2 * (dy - 1) + dc, rest))


def halves(x):
    hi = x.astype(BF16)
    return hi, (x - hi.astype(F32)).astype(BF16)


def dot_nt(a, b):
    return lax.dot_general(a, b, (((1,), (1,)), ((), ())), preferred_element_type=F32)


def dot_nn(a, b):
    return lax.dot_general(a, b, (((1,), (0,)), ((), ())), preferred_element_type=F32)


def kernel(
    groups, cols, bounds_ref, labels_ref, points_hbm, cent_hbm, out_ref,
    points_ref, cent_ref, seats_ref, rows_ref, xh_ref, xl_ref, logit_ref, valid_ref, share_ref, code_ref, stat_ref,
    w_ref, i_ref, j_ref, t_ref, rr_ref, rl_ref, sr_ref, sl_ref,
    cw_ref, ci_ref, crr_ref, crl_ref, csr_ref, csl_ref,
    send_sem, recv_sem, local_sem, fan_sem, right_sem, left_sem, relay_sem, far_sem,
    met_sem, stat_send, stat_recv, pair_send, pair_recv, chain_send, chain_recv,
):
    side = plane_side(groups)
    parts = side + 1
    rows_dev, width = points_ref.shape
    kids = cent_ref.shape[0]
    half_kids = kids // 2
    tile = width // LANES
    chunks = width // CHUNK
    block = SEATS * tile
    seat_count = groups * SEATS
    all_rows = cols * seat_count
    score_scale = SHARPNESS / width
    me = lax.axis_index("grp")
    col = lax.axis_index("col")
    core = me % 2
    sibling = me + 1 - 2 * core
    ahead = lax.rem(me + 2, groups)
    behind = lax.rem(me + groups - 2, groups)
    right, left = lax.rem(col + 1, cols), lax.rem(col + cols - 1, cols)
    far = lax.rem(col + 2, cols)

    barrier = pltpu.get_barrier_semaphore()
    for k in range(2):
        for step in range(part_steps(k, side)):
            if k or step:
                to = peer(me, k, step, side)
                pl.semaphore_signal(barrier, inc=1, device_id=(to, col), device_id_type=MESH)
    for other in (right, left, far):
        pl.semaphore_signal(barrier, inc=1, device_id=(me, other), device_id_type=MESH)

    points_copy = pltpu.make_async_copy(points_hbm, points_ref, local_sem.at[0])
    cent_copy = pltpu.make_async_copy(cent_hbm, cent_ref, local_sem.at[1])
    points_copy.start()
    cent_copy.start()

    mine = labels_ref[...].astype(F32)
    labels = jnp.broadcast_to(mine, (rows_dev, rows_dev))
    r = lax.broadcasted_iota(jnp.int32, (rows_dev, rows_dev), 0)
    c = lax.broadcasted_iota(jnp.int32, (rows_dev, rows_dev), 1)
    before = (labels == labels.T) & (r < c)
    rank = jnp.sum(before.astype(F32), axis=0, keepdims=True)
    first = jnp.zeros_like(mine)
    for p in range(bounds_ref.shape[0] - 1):
        first = jnp.where(mine == p, bounds_ref[p].astype(F32), first)
    seat = (first * SEATS + rank).astype(jnp.int32)
    seat = SEATS * tour_place(me, lax.shift_right_logical(seat, 1), side) + (seat & 1)
    s = lax.broadcasted_iota(jnp.int32, (seat_count, rows_dev), 0)
    pick = (s == jnp.broadcast_to(seat, (seat_count, rows_dev))).astype(F32)
    empty = 1.0 - jnp.sum(pick, axis=1, keepdims=True)
    lane = lax.broadcasted_iota(jnp.int32, (seat_count, LANES), 1)
    points_copy.wait()
    for q in range(tile):
        part = jnp.dot(pick, points_ref[:, q * LANES : (q + 1) * LANES], precision=HIGHEST)
        if q == 0:
            part = part + jnp.where(lane == 0, empty * MARK, 0.0)
        seats_ref[pl.ds(q, seat_count, stride=tile), :] = part

    pl.semaphore_wait(barrier, 4 * side - 3 + 3)
    for dy in range(side - 1):
        to = peer(me, 1, 2 * dy, side)
        pl.semaphore_signal(met_sem, inc=1, device_id=(to, col), device_id_type=MESH)

    def part_rows(k):
        return part_steps(k, side) * block

    def place(k, source, lo, size):
        base = cols * part_first(k, side) * block + source * part_rows(k) + lo
        return rows_ref.at[pl.ds(pl.multiple_of(base, 8), size), :]

    def seated(k, step):
        return seats_ref.at[pl.ds(pl.multiple_of((part_first(k, side) + step) * block, block), block), :]

    def send_part(k):
        def send(step, carry):
            to = peer(me, k, step, side)
            pltpu.make_async_remote_copy(
                src_ref=seated(k, step),
                dst_ref=place(k, col, step * block, block),
                send_sem=send_sem.at[k],
                recv_sem=recv_sem.at[k],
                device_id=(to, col),
                device_id_type=MESH,
            ).start()
            return carry

        lax.fori_loop(0 if k else 1, part_steps(k, side), send, 0)

    def own_copy():
        return pltpu.make_async_copy(seated(0, 0), place(0, col, 0, block), local_sem.at[2])

    def link(src, dst, ssem, rsem, to):
        return pltpu.make_async_remote_copy(
            src_ref=src, dst_ref=dst, send_sem=ssem, recv_sem=rsem,
            device_id=to, device_id_type=MESH,
        )

    def piece(k, source, n):
        half = part_rows(k) // 2
        return place(k, source, n * half, half)

    def to_right(k, source, n):
        cut = piece(k, source, n)
        return link(cut, cut, fan_sem.at[0, n, k], right_sem.at[n, k], (me, right))

    def to_left(k, source, n):
        cut = piece(k, source, n)
        return link(cut, cut, fan_sem.at[1, n, k], left_sem.at[n, k], (me, left))

    def on_right(k, source):
        cut = piece(k, source, 0)
        return link(cut, cut, relay_sem.at[0, k], far_sem.at[0, k], (me, right))

    def on_left(k, source):
        cut = piece(k, source, 1)
        return link(cut, cut, relay_sem.at[1, k], far_sem.at[1, k], (me, left))

    def arrived(k):
        lo = 0 if k else block
        cut = place(k, col, lo, part_rows(k) - lo)
        link(cut, cut, send_sem.at[k], recv_sem.at[k], (me, right)).wait_recv()

    def fan(k):
        to_right(k, col, 0).start()
        to_left(k, col, 1).start()
        to_right(k, col, 1).start()
        to_left(k, col, 0).start()

    def relay(k):
        to_right(k, left, 0).wait_recv()
        on_right(k, left).start()
        to_left(k, right, 1).wait_recv()
        on_left(k, right).start()

    def settled(k):
        to_right(k, left, 1).wait_recv()
        to_left(k, right, 0).wait_recv()
        on_right(k, far).wait_recv()
        on_left(k, far).wait_recv()

    def encode(d, block_of_c):
        hi, lo = halves(block_of_c)
        code_ref[d, :kids, :] = hi
        code_ref[d, kids:, :] = lo

    def score(d, lo, size):
        a = dot_nt(code_ref[d], xh_ref[d, lo : lo + size, :])
        b = dot_nt(code_ref[d, :kids, :], xl_ref[d, lo : lo + size, :])
        return a[:kids] + a[kids:] + b

    pick_mark = (
        (lax.broadcasted_iota(jnp.int32, (16, CHUNK), 0) == 0)
        & (lax.broadcasted_iota(jnp.int32, (16, CHUNK), 1) == 0)
    ).astype(BF16)
    batch = 2 * rows_dev
    spans = [(b * batch, batch) for b in range(all_rows // batch)]
    early_spans = spans[:-1] + [(spans[-1][0] + n * rows_dev, rows_dev) for n in range(2)]
    last_part = [
        min(k for k in range(parts) if cols * SEATS * part_first(k + 1, side) >= lo + size) for lo, size in early_spans
    ]

    def summarize(it, lo, size, half_norm):
        cut = slice(lo, lo + size)
        logits = (logit_ref[:, cut] - half_norm) * score_scale
        peak = jnp.max(logits, axis=0, keepdims=True)
        raised = jnp.exp(logits - peak)
        logit_ref[:, cut] = raised
        stat_ref[it, 0, 0:1, cut] = peak
        stat_ref[it, 0, 1:2, cut] = jnp.sum(raised, axis=0, keepdims=True)

    def absorb(lo, size):
        for q in range(tile):
            hi, rest = halves(rows_ref[pl.ds(lo * tile + q, size, stride=tile), :])
            d, at = q // (CHUNK // LANES), (q % (CHUNK // LANES)) * LANES
            xh_ref[d, lo : lo + size, at : at + LANES] = hi
            xl_ref[d, lo : lo + size, at : at + LANES] = rest
        total = score(0, lo, size)
        for d in range(1, chunks):
            total = total + score(d, lo, size)
        logit_ref[:, lo : lo + size] = total
        mark = dot_nt(pick_mark, xh_ref[0, lo : lo + size, :])[0:1]
        valid_ref[:, lo : lo + size] = (mark < 0.5 * MARK).astype(F32)
        summarize(0, lo, size, half_norm)

    send_part(0)
    send_part(1)
    own_copy().start()
    cent_copy.wait()
    half_norm = jnp.zeros((kids, 1), F32)
    for d in range(chunks):
        now = cent_ref[:, d * CHUNK : (d + 1) * CHUNK]
        encode(d, now)
        half_norm = half_norm + 0.5 * jnp.sum(now * now, axis=1, keepdims=True)

    pl.semaphore_wait(met_sem, side - 1)
    for k in range(2, 2 + WINDOW):
        send_part(k)
    own_copy().wait()
    for k in range(parts):
        arrived(k)
        fan(k)
        if k >= 1 and k + 1 + WINDOW < parts:
            send_part(k + 1 + WINDOW)
        if k >= 1:
            relay(k - 1)
        if k >= 2:
            settled(k - 2)
        if k - 2 in last_part:
            absorb(*early_spans[last_part.index(k - 2)])
    relay(parts - 1)
    for k in (parts - 2, parts - 1):
        settled(k)
        for span, last in zip(early_spans, last_part):
            if last == k:
                absorb(*span)

    chip = me // 2

    def owner(g):
        count = jnp.zeros((), jnp.int32)
        for p in range(1, bounds_ref.shape[0]):
            count = count + (bounds_ref[p] <= g).astype(jnp.int32)
        return count

    owner0, owner1 = owner(2 * chip), owner(2 * chip + 1)
    same = (owner0 == owner1).astype(F32)
    from_left = ((owner(2 * chip - 1) == owner0) & (chip > 0)).astype(F32)
    from_right = (owner(2 * chip + 2) == owner1).astype(F32)
    through_left, through_right = same * from_left, same * from_right
    is0 = core == 0
    mine_left = jnp.where(is0, from_left, through_left)
    mine_right = jnp.where(is0, through_right, from_right)
    other_left = jnp.where(is0, through_left, from_left)
    other_right = jnp.where(is0, from_right, through_right)
    my_half = pl.multiple_of(core * half_kids, half_kids)
    its_half = pl.multiple_of((1 - core) * half_kids, half_kids)

    for it in range(ITERS):
        stats = [
            link(stat_ref.at[it, 0], stat_ref.at[it, 1 + n], stat_send.at[it, n], stat_recv.at[it, n], (me, to))
            for n, to in enumerate((right, left, far))
        ]
        for copy in stats:
            copy.start()
        for copy in stats:
            copy.wait()
        peak = stat_ref[it, 0, 0:1, :]
        top = peak
        for n in range(3):
            top = jnp.maximum(top, stat_ref[it, 1 + n, 0:1, :])
        denominator = jnp.zeros((1, all_rows), F32)
        for n in range(4):
            denominator = denominator + stat_ref[it, n, 1:2, :] * jnp.exp(stat_ref[it, n, 0:1, :] - top)
        scale = valid_ref[...] * jnp.exp(peak - top) / denominator
        shares = logit_ref[...] * scale
        hi, lo = halves(shares)
        share_ref[:kids, :] = hi
        share_ref[kids:, :] = lo
        counted = dot_nt(jnp.ones((16, all_rows), BF16), share_ref[...])[:8]
        cw_ref[it, 0] = counted[:, :kids] + counted[:, kids:]

        def bufs(n):
            if n == 0:
                refs = (cw_ref, ci_ref, ci_ref, ci_ref, crr_ref, crl_ref, csr_ref, csl_ref)
                return [ref.at[it, 0] for ref in refs]
            refs = (w_ref, i_ref, j_ref, t_ref, rr_ref, rl_ref, sr_ref, sl_ref)
            return [ref.at[it, n - 1] for ref in refs]

        def swap(n):
            w, i = bufs(n)[:2]
            src = w.at[pl.ds(its_half, half_kids), :] if n else w
            return link(src, i, pair_send.at[it, 0, n], pair_recv.at[it, 0, n], (sibling, col))

        def swap_back(n):
            j, t = bufs(n)[2:4]
            return link(t, j, pair_send.at[it, 1, n], pair_recv.at[it, 1, n], (sibling, col))

        def shift_right(n, m):
            b = bufs(n)
            return link(b[6].at[m], b[4].at[m], chain_send.at[it, 0, n, m], chain_recv.at[it, 0, n, m], (ahead, col))

        def shift_left(n, m):
            b = bufs(n)
            return link(b[7].at[m], b[5].at[m], chain_send.at[it, 1, n, m], chain_recv.at[it, 1, n, m], (behind, col))

        def begin(n):
            swap(n).wait_recv()
            b = bufs(n)
            own = b[0][pl.ds(my_half, half_kids), :] if n else b[0][...]
            its = b[1][...]
            b[7][0] = jnp.where(is0, own + same * its, its + same * own)
            b[6][0] = jnp.where(is0, its + same * own, own + same * its)
            shift_right(n, 0).start()
            shift_left(n, 0).start()

        swap(0).start()
        for d in range(chunks):
            both = dot_nn(share_ref[...], xh_ref[d])
            rest = dot_nn(share_ref[:kids, :], xl_ref[d])
            w_ref[it, d] = both[:kids] + both[kids:] + rest
            swap(d + 1).start()
            begin(d)
        begin(chunks)
        for m in range(ROUNDS - 1):
            for n in range(chunks + 1):
                b = bufs(n)
                shift_right(n, m).wait_recv()
                b[6][m + 1] = b[6][0] + through_left * b[4][m]
                shift_right(n, m + 1).start()
                shift_left(n, m).wait_recv()
                b[7][m + 1] = b[7][0] + through_right * b[5][m]
                shift_left(n, m + 1).start()
        for n in range(chunks + 1):
            b = bufs(n)
            shift_right(n, ROUNDS - 1).wait_recv()
            shift_left(n, ROUNDS - 1).wait_recv()
            from_l, from_r = b[4][ROUNDS - 1], b[5][ROUNDS - 1]
            toward0, toward1 = b[7][0], b[6][0]
            if n == 0:
                count = jnp.where(is0, toward0, toward1) + mine_left * from_l + mine_right * from_r
                continue
            b[3][...] = jnp.where(is0, toward1, toward0) + other_left * from_l + other_right * from_r
            swap_back(n).start()
            b[0][pl.ds(my_half, half_kids), :] = (
                jnp.where(is0, toward0, toward1) + mine_left * from_l + mine_right * from_r
            )
        swap(0).wait_send()
        shrink = 1.0 / (jnp.broadcast_to(count[0:1, :], (kids, kids)).T + 1.0)
        shrink = jnp.concatenate([shrink] * (CHUNK // kids), axis=1)
        source = cent_ref if it == 0 else out_ref
        half_norm = jnp.zeros((kids, 1), F32)
        for d in range(chunks):
            swap(d + 1).wait_send()
            swap_back(d + 1).wait_recv()
            w_ref[it, d, pl.ds(its_half, half_kids), :] = j_ref[it, d]
            at = slice(d * CHUNK, (d + 1) * CHUNK)
            now = (w_ref[it, d] + source[:, at]) * shrink
            out_ref[:, at] = now
            if it + 1 < ITERS:
                encode(d, now)
                half_norm = half_norm + 0.5 * jnp.sum(now * now, axis=1, keepdims=True)
                for lo, size in spans:
                    scored = score(d, lo, size)
                    if d > 0:
                        scored = scored + logit_ref[:, lo : lo + size]
                    logit_ref[:, lo : lo + size] = scored
                    if d == chunks - 1:
                        summarize(it + 1, lo, size, half_norm)
        for n in range(chunks + 1):
            if n:
                swap_back(n).wait_send()
            for m in range(ROUNDS):
                shift_right(n, m).wait_send()
                shift_left(n, m).wait_send()

    for k in range(parts):
        for n in range(2):
            to_right(k, col, n).wait_send()
            to_left(k, col, n).wait_send()
        on_right(k, left).wait_send()
        on_left(k, right).wait_send()
        lo = 0 if k else block
        sent = place(k, col, lo, part_rows(k) - lo)
        link(sent, sent, send_sem.at[k], recv_sem.at[k], (me, right)).wait_send()


def on_device(points, labels, boundaries, centroids):
    groups = lax.axis_size("grp")
    cols = lax.axis_size("col")
    rows, width = points.shape
    kids = centroids.shape[1]
    tile = width // LANES
    side = plane_side(groups)
    parts = side + 1
    seat_count = groups * SEATS
    all_rows = cols * seat_count
    chunks = width // CHUNK
    dma = pltpu.SemaphoreType.DMA
    vmem = pl.BlockSpec(memory_space=pltpu.VMEM)
    in_hbm = pl.BlockSpec(memory_space=pl.ANY)

    half = kids // 2
    one = pltpu.VMEM((ITERS, chunks, half, CHUNK), F32)
    many = pltpu.VMEM((ITERS, chunks, ROUNDS, half, CHUNK), F32)
    few = pltpu.VMEM((ITERS, 1, 8, kids), F32)
    few_rounds = pltpu.VMEM((ITERS, 1, ROUNDS, 8, kids), F32)

    out = pl.pallas_call(
        functools.partial(kernel, groups, cols),
        out_shape=jax.ShapeDtypeStruct((kids, width), F32),
        in_specs=[pl.BlockSpec(memory_space=pltpu.SMEM), vmem, in_hbm, in_hbm],
        out_specs=vmem,
        scratch_shapes=[
            pltpu.VMEM((rows, width), F32),
            pltpu.VMEM((kids, width), F32),
            pltpu.VMEM((seat_count * tile, LANES), F32),
            pltpu.VMEM((all_rows * tile, LANES), F32),
            pltpu.VMEM((chunks, all_rows, CHUNK), BF16),
            pltpu.VMEM((chunks, all_rows, CHUNK), BF16),
            pltpu.VMEM((kids, all_rows), F32),
            pltpu.VMEM((1, all_rows), F32),
            pltpu.VMEM((2 * kids, all_rows), BF16),
            pltpu.VMEM((chunks, 2 * kids, CHUNK), BF16),
            pltpu.VMEM((ITERS, 4, 2, all_rows), F32),
            pltpu.VMEM((ITERS, chunks, kids, CHUNK), F32), one, one, one, many, many, many, many,
            few, few, few_rounds, few_rounds, few_rounds, few_rounds,
            dma((parts,)), dma((parts,)), dma((3,)), dma((2, 2, parts)), dma((2, parts)), dma((2, parts)),
            dma((2, parts)), dma((2, parts)),
            pltpu.SemaphoreType.REGULAR,
            dma((ITERS, 3)), dma((ITERS, 3)),
            dma((ITERS, 2, chunks + 1)), dma((ITERS, 2, chunks + 1)),
            dma((ITERS, 2, chunks + 1, ROUNDS)), dma((ITERS, 2, chunks + 1, ROUNDS)),
        ],
        compiler_params=pltpu.CompilerParams(
            collective_id=0, has_side_effects=True, vmem_limit_bytes=56 << 20
        ),
    )(boundaries, labels.reshape(1, rows), points, centroids[0])
    return out[None]


def solution(mesh):
    placed = (P(("grp", "col"), None), P(("grp", "col")), P(), P("grp", "col", None))
    return jax.shard_map(
        on_device, mesh=mesh, in_specs=placed, out_specs=P("grp", "col", None), check_vma=False
    )
```

time: 135 us -> 121 us (0.90)
  Pallas kernels: 131 us -> 119 us
  local copies, waits for them, and re-layouts: 4.18 us -> 1.89 us
    pallas_call x1, Pallas kernels: 131 us -> 119 us  [on_device(): pl.pallas_call(functools.partial(kernel, groups, cols), out_shape=jax.Sha...]
    unnamed x9 -> x1, local copies, waits for them, and re-layouts: 4.18 us -> 1.89 us
where the time goes in v2:
time: 121 us
  Pallas kernels  119 us (98%)
  local copies, waits for them, and re-layouts  1.89 us (2%)
    pallas_call x1, Pallas kernels, on_device(): pl.pallas_call(functools.partial(kernel, groups, cols), out_shape=jax.Sha...  119 us

profile of v2, /device:TPU:1, one launch (start us, length us, event | category | flops | bytes accessed | tf_op | source)
XLA Modules:
  0.0 120.7 jit_solution(6721064995693896684)
XLA Ops:
  0.0 118.8 %shard_map.46 = f32[128,1024]{1,0:T(8,128)} custom-call(s32[33]{0:T(128)} %bounds_ref.1, s32[1,128]{1,0:T(1,128)} %bitcast.5, f32[128,1024]{1,0:T(8,128)} %points_hbm.1, f32[128,1024]{1,0:T(8,128)} %bitcast.4), custom_call_target="tpu_custom_call" | custom-call | tf_op jit(solution)/shard_map/pallas_call | solution.py:468
  118.8 1.9 %copy.6 = f32[1,128,1024]{2,1,0:T(8,128)} copy(f32[1,128,1024]{2,1,0:T(8,128)} %bitcast.3) | data formatting | bytes 1048576

commit v3 on v2

--- a/solution.py
+++ b/solution.py
@@ -15,7 +15,7 @@
 SEATS = 2
 MARK = 4096.0
 ROUNDS = 3
-WINDOW = 3
+WINDOW = 4
 CHUNK = 256
 F32 = jnp.float32
 BF16 = jnp.bfloat16
@@ -74,7 +74,7 @@
 
 def kernel(
     groups, cols, bounds_ref, labels_ref, points_hbm, cent_hbm, out_ref,
-    points_ref, cent_ref, seats_ref, rows_ref, xh_ref, xl_ref, logit_ref, valid_ref, share_ref, code_ref, stat_ref,
+    points_ref, cent_ref, seats_ref, early_ref, rows_ref, xh_ref, xl_ref, logit_ref, valid_ref, share_ref, code_ref, stat_ref,
     w_ref, i_ref, j_ref, t_ref, rr_ref, rl_ref, sr_ref, sl_ref,
     cw_ref, ci_ref, crr_ref, crl_ref, csr_ref, csl_ref,
     send_sem, recv_sem, local_sem, fan_sem, right_sem, left_sem, relay_sem, far_sem,
@@ -148,6 +148,8 @@
         base = cols * part_first(k, side) * block + source * part_rows(k) + lo
         return rows_ref.at[pl.ds(pl.multiple_of(base, 8), size), :]
 
+    last = parts - 1
+
     def seated(k, step):
         return seats_ref.at[pl.ds(pl.multiple_of((part_first(k, side) + step) * block, block), block), :]
 
@@ -166,6 +168,18 @@
 
         lax.fori_loop(0 if k else 1, part_steps(k, side), send, 0)
 
+    def send_gathered(source):
+        def send(step, carry):
+            to = peer(me, last, step, side)
+            link(
+                early_ref.at[source, pl.ds(pl.multiple_of(step * block, block), block), :],
+                place(last, source, step * block, block),
+                send_sem.at[last], recv_sem.at[last], (to, col),
+            ).start()
+            return carry
+
+        lax.fori_loop(0, part_steps(last, side), send, 0)
+
     def own_copy():
         return pltpu.make_async_copy(seated(0, 0), place(0, col, 0, block), local_sem.at[2])
 
@@ -177,15 +191,21 @@
 
     def piece(k, source, n):
         half = part_rows(k) // 2
+        if k == last:
+            return early_ref.at[source, pl.ds(n * half, half), :]
         return place(k, source, n * half, half)
 
+    def start_piece(k, source, n):
+        half = part_rows(k) // 2
+        if k == last:
+            return seats_ref.at[pl.ds(part_first(k, side) * block + n * half, half), :]
+        return piece(k, source, n)
+
     def to_right(k, source, n):
-        cut = piece(k, source, n)
-        return link(cut, cut, fan_sem.at[0, n, k], right_sem.at[n, k], (me, right))
+        return link(start_piece(k, source, n), piece(k, source, n), fan_sem.at[0, n, k], right_sem.at[n, k], (me, right))
 
     def to_left(k, source, n):
-        cut = piece(k, source, n)
-        return link(cut, cut, fan_sem.at[1, n, k], left_sem.at[n, k], (me, left))
+        return link(start_piece(k, source, n), piece(k, source, n), fan_sem.at[1, n, k], left_sem.at[n, k], (me, left))
 
     def on_right(k, source):
         cut = piece(k, source, 0)
@@ -195,9 +215,14 @@
         cut = piece(k, source, 1)
         return link(cut, cut, relay_sem.at[1, k], far_sem.at[1, k], (me, left))
 
+    def moved(k):
+        if k == last:
+            return rows_ref.at[pl.ds(cols * part_first(k, side) * block, cols * part_rows(k)), :]
+        lo = 0 if k else block
+        return place(k, col, lo, part_rows(k) - lo)
+
     def arrived(k):
-        lo = 0 if k else block
-        cut = place(k, col, lo, part_rows(k) - lo)
+        cut = moved(k)
         link(cut, cut, send_sem.at[k], recv_sem.at[k], (me, right)).wait_recv()
 
     def fan(k):
@@ -262,6 +287,7 @@
         valid_ref[:, lo : lo + size] = (mark < 0.5 * MARK).astype(F32)
         summarize(0, lo, size, half_norm)
 
+    fan(last)
     send_part(0)
     send_part(1)
     own_copy().start()
@@ -276,23 +302,38 @@
     for k in range(2, 2 + WINDOW):
         send_part(k)
     own_copy().wait()
-    for k in range(parts):
+    relay(last)
+    for k in range(last):
         arrived(k)
         fan(k)
-        if k >= 1 and k + 1 + WINDOW < parts:
-            send_part(k + 1 + WINDOW)
+        if k == 1:
+            for later in range(2 + WINDOW, last):
+                send_part(later)
+            settled(last)
+        if k == 2:
+            send_part(last)
+        if k == 3:
+            send_gathered(left)
+        if k == 4:
+            send_gathered(right)
+        if k == 5:
+            send_gathered(far)
         if k >= 1:
             relay(k - 1)
         if k >= 2:
             settled(k - 2)
         if k - 2 in last_part:
             absorb(*early_spans[last_part.index(k - 2)])
-    relay(parts - 1)
-    for k in (parts - 2, parts - 1):
-        settled(k)
-        for span, last in zip(early_spans, last_part):
-            if last == k:
-                absorb(*span)
+    relay(last - 1)
+    settled(last - 2)
+    for span, need in zip(early_spans, last_part):
+        if need == last - 2:
+            absorb(*span)
+    settled(last - 1)
+    arrived(last)
+    for span, need in zip(early_spans, last_part):
+        if need > last - 2:
+            absorb(*span)
 
     chip = me // 2
 
@@ -439,8 +480,7 @@
             to_left(k, col, n).wait_send()
         on_right(k, left).wait_send()
         on_left(k, right).wait_send()
-        lo = 0 if k else block
-        sent = place(k, col, lo, part_rows(k) - lo)
+        sent = moved(k)
         link(sent, sent, send_sem.at[k], recv_sem.at[k], (me, right)).wait_send()
 
 
@@ -474,6 +514,7 @@
             pltpu.VMEM((rows, width), F32),
             pltpu.VMEM((kids, width), F32),
             pltpu.VMEM((seat_count * tile, LANES), F32),
+            pltpu.VMEM((cols, part_steps(parts - 1, side) * SEATS * tile, LANES), F32),
             pltpu.VMEM((all_rows * tile, LANES), F32),
             pltpu.VMEM((chunks, all_rows, CHUNK), BF16),
             pltpu.VMEM((chunks, all_rows, CHUNK), BF16),

time: 121 us -> 117 us (0.967)
  Pallas kernels: 119 us -> 115 us
    pallas_call x1, Pallas kernels: 119 us -> 115 us  [on_device(): pl.pallas_call(functools.partial(kernel, groups, cols), out_shape=jax.Sha...]
where the time goes in v3:
time: 117 us
  Pallas kernels  115 us (98%)
  local copies, waits for them, and re-layouts  1.89 us (2%)
    pallas_call x1, Pallas kernels, on_device(): pl.pallas_call(functools.partial(kernel, groups, cols), out_shape=jax.Sha...  115 us

profile of v3, /device:TPU:1, one launch (start us, length us, event | category | flops | bytes accessed | tf_op | source)
XLA Modules:
  0.0 117.1 jit_solution(18028205282273726605)
XLA Ops:
  0.0 115.2 %shard_map.46 = f32[128,1024]{1,0:T(8,128)} custom-call(s32[33]{0:T(128)} %bounds_ref.1, s32[1,128]{1,0:T(1,128)} %bitcast.5, f32[128,1024]{1,0:T(8,128)} %points_hbm.1, f32[128,1024]{1,0:T(8,128)} %bitcast.4), custom_call_target="tpu_custom_call" | custom-call | tf_op jit(solution)/shard_map/pallas_call | solution.py:508
  115.2 1.9 %copy.6 = f32[1,128,1024]{2,1,0:T(8,128)} copy(f32[1,128,1024]{2,1,0:T(8,128)} %bitcast.3) | data formatting | bytes 1048576

commit v4 on v3

--- a/solution.py
+++ b/solution.py
@@ -513,9 +513,9 @@
         scratch_shapes=[
             pltpu.VMEM((rows, width), F32),
             pltpu.VMEM((kids, width), F32),
-            pltpu.VMEM((seat_count * tile, LANES), F32),
+            pltpu.VMEM((seat_count * tile + tile, LANES), F32),
             pltpu.VMEM((cols, part_steps(parts - 1, side) * SEATS * tile, LANES), F32),
-            pltpu.VMEM((all_rows * tile, LANES), F32),
+            pltpu.VMEM((all_rows * tile + tile, LANES), F32),
             pltpu.VMEM((chunks, all_rows, CHUNK), BF16),
             pltpu.VMEM((chunks, all_rows, CHUNK), BF16),
             pltpu.VMEM((kids, all_rows), F32),

time: 117 us -> 117 us (level)
  no operation moved by 1% of the time
where the time goes in v4:
time: 117 us
  Pallas kernels  115 us (98%)
  local copies, waits for them, and re-layouts  1.89 us (2%)
    pallas_call x1, Pallas kernels, on_device(): pl.pallas_call(functools.partial(kernel, groups, cols), out_shape=jax.Sha...  115 us

profile of v4, /device:TPU:1, one launch (start us, length us, event | category | flops | bytes accessed | tf_op | source)
XLA Modules:
  0.0 117.1 jit_solution(3935344126937085648)
XLA Ops:
  0.0 115.2 %shard_map.46 = f32[128,1024]{1,0:T(8,128)} custom-call(s32[33]{0:T(128)} %bounds_ref.1, s32[1,128]{1,0:T(1,128)} %bitcast.5, f32[128,1024]{1,0:T(8,128)} %points_hbm.1, f32[128,1024]{1,0:T(8,128)} %bitcast.4), custom_call_target="tpu_custom_call" | custom-call | tf_op jit(solution)/shard_map/pallas_call | solution.py:508
  115.2 1.9 %copy.6 = f32[1,128,1024]{2,1,0:T(8,128)} copy(f32[1,128,1024]{2,1,0:T(8,128)} %bitcast.3) | data formatting | bytes 1048576
